TPU v7x, 32 devices: a whole 2x2x4 slice. The times are simulated.
32 devices in a mesh: layer: 4 (over y, core), lat: 8 (over z, x).
Axes of the slice: x: 2, y: 2, z: 4, core: 2. Of those that a mesh axis runs over, the one named last changes fastest.
Arguments:
- resid_halves: bfloat16 [4, 1024, 4096], P('layer'), may hold values from -6 to 6
- enc_weight: bfloat16 [4, 4096, 16384], P('layer', None, 'lat'), may hold values from -0.0625 to 0.0625
- enc_bias: float32 [2, 16384], P(None, 'lat'), may hold values from -3 to 3
- jump_threshold: float32 [2, 16384], P(None, 'lat'), may hold values from 0.1 to 1
- dec_weight: bfloat16 [4, 2, 16384, 8192], P('layer', None, 'lat'), may hold values from -0.03125 to 0.03125
- dec_bias: float32 [4, 8192], P('layer'), may hold values from -3 to 3
- clamp_rows: int32 [2, 1024], replicated, may hold values from 0 to 1023, each once within a row
- clamp_feats: int32 [2, 1024], replicated, may hold values from 0 to 16383
- clamp_slots: int32 [2, 1024], replicated, may hold values from 0 to 15
- clamp_values: float32 [16], replicated, may hold values from 5 to 15
Outputs:
- recon: bfloat16 [4, 1024, 8192], P('layer', 'lat')
Inputs may be any that keep to these rules, and one draw needn't show every extreme that they name: Each row of clamp_rows names every token row once.
All inputs are finite; a program needn't handle non-finite values.
Results may differ from a plain program's by a relative error of at most 0.0042.
Values may be sent and summed in bfloat16 or wider, within the bound.
A program may use at most 192 MiB of HBM per device.

v0:
```python
import jax
import jax.numpy as jnp
from jax import lax
from jax.sharding import PartitionSpec as P


def swapped(value, axis, distance):
    mask = 2**distance
    pairs = [(source, source ^ mask) for source in range(lax.axis_size(axis))]
    return lax.ppermute(value, axis, pairs)


def clamp_codes(activity, feat_ids, slot_ids, row_ids, clamp_values, lat_first):
    n_rows = activity.shape[0]
    width = activity.shape[1]
    row_hot = (row_ids[:, None] == jnp.arange(n_rows, dtype=jnp.int32)[None, :]).astype(jnp.float32)
    slot_hot = (
        slot_ids[:, None] == jnp.arange(clamp_values.shape[0], dtype=jnp.int32)[None, :]
    ).astype(jnp.float32)
    chosen = jnp.dot(slot_hot, clamp_values, precision=lax.Precision.HIGHEST)
    feat_row = jnp.dot(feat_ids.astype(jnp.float32), row_hot, precision=lax.Precision.HIGHEST)
    value_row = jnp.dot(chosen, row_hot, precision=lax.Precision.HIGHEST)
    target_col = feat_row.astype(jnp.int32) - lat_first
    hit = target_col[:, None] == jnp.arange(width, dtype=jnp.int32)[None, :]
    return jnp.where(hit, value_row[:, None], activity)


def shards(
    resid_halves,
    enc_weight,
    enc_bias,
    jump_threshold,
    dec_weight,
    dec_bias,
    clamp_rows,
    clamp_feats,
    clamp_slots,
    clamp_values,
):
    group = lax.axis_index("layer")
    source = group // 2
    shard_width = enc_weight.shape[2]
    lat_first = lax.axis_index("lat") * shard_width
    my_bias = lax.dynamic_index_in_dim(enc_bias, source, 0, keepdims=False)
    my_thresh = lax.dynamic_index_in_dim(jump_threshold, source, 0, keepdims=False)
    my_feats = lax.dynamic_index_in_dim(clamp_feats, source, 0, keepdims=False)
    my_slots = lax.dynamic_index_in_dim(clamp_slots, source, 0, keepdims=False)
    my_rows = lax.dynamic_index_in_dim(clamp_rows, source, 0, keepdims=False)
    partial_pre = jnp.dot(resid_halves[0], enc_weight[0], preferred_element_type=jnp.float32)
    partner = swapped(partial_pre, "layer", 0)
    pre_act = partial_pre + partner + my_bias[None, :]
    ramp = jnp.clip((pre_act - my_thresh[None, :]) / 0.25 + 1.0, 0.0, 1.0)
    clamped = clamp_codes(pre_act * ramp, my_feats, my_slots, my_rows, clamp_values, lat_first)
    own_codes = clamped.astype(jnp.bfloat16)
    other_codes = swapped(own_codes, "layer", 1)
    both_codes = jnp.where(
        source == 0, jnp.stack([own_codes, other_codes]), jnp.stack([other_codes, own_codes])
    )
    total = jnp.dot(both_codes[0], dec_weight[0, 0], preferred_element_type=jnp.float32)
    summed = lax.psum_scatter(
        total + jnp.dot(both_codes[1], dec_weight[0, 1], preferred_element_type=jnp.float32),
        "lat",
        scatter_dimension=0,
        tiled=True,
    )
    result = (summed + dec_bias[0][None, :]).astype(jnp.bfloat16)
    return result[None, :, :]


def solution(mesh):
    return jax.shard_map(
        shards,
        mesh=mesh,
        in_specs=(
            P("layer", None, None),
            P("layer", None, "lat"),
            P(None, "lat"),
            P(None, "lat"),
            P("layer", None, "lat", None),
            P("layer", None),
            P(),
            P(),
            P(),
            P(),
        ),
        out_specs=P("layer", "lat", None),
        check_vma=False,
    )
```

profile of v0, /device:TPU:0, one launch (start us, length us, event | category | flops | bytes accessed | tf_op | source)
XLA Modules:
  0.0 802.0 jit_solution(12650758169183267858)
XLA Ops:
  6.5 0.0 copy-start
  6.5 0.0 copy-start.6
  6.5 0.0 copy-start.7
  6.5 0.0 copy-start.8
  6.5 0.0 copy-start.4
  6.5 0.0 copy-start.5
  6.6 0.0 reduce-scatter.2.cloned.1.call-start
  6.6 24.1 %fusion.9 = f32[1024,2048]{1,0:T(8,128)} fusion(bf16[1,4096,2048]{2,1,0:T(8,128)(2,1)} %param.11, bf16[1,1024,4096]{2,1,0:T(8,128)(2,1)} %param.10), kind=kOutput, calls=%fused_computation.7 | convolution fusion | flops 17179869184 | bytes 33554432 | tf_op jit(solution)/shard_map/dot_general | solution.py:49
  30.7 0.5 collective-permute-start
  31.1 0.0 copy-done.6
  31.1 0.0 copy-done.7
  31.2 0.0 copy-done.8
  31.2 1.5 fusion.13
  32.6 0.0 copy-done
  32.6 0.4 convolution_bitcast_fusion
  33.1 1.5 fusion.12
  34.6 0.0 copy-done.4
  34.6 0.0 copy-done.5
  34.6 9.7 %collective-permute-done = f32[1024,2048]{1,0:T(8,128)} collective-permute-done((f32[1024,2048]{1,0:T(8,128)}, f32[1024,2048]{1,0:T(8,128)}, u32[]{:S(2)}, u32[]{:S(2)}) %collective-permute-start) | collective-permute-done | bytes 8388640 | tf_op jit(solution)/shard_map/ppermute | solution.py:10
  44.3 8.7 %select_convert_fusion = bf16[1024,2048]{1,0:T(8,128)(2,1)} fusion(f32[1024,2048]{1,0:T(8,128)} %fusion.9, f32[1024,2048]{1,0:T(8,128)} %collective-permute-done, f32[2048]{0:T(1024)S(1)} %bitcast.43, f32[2048]{0:T(1024)S(1)} %bitcast.44, f32[1024]{0:T(1024)S(1)} %bitcast.49, s32[1024]{0:T(1024)S(1)} %convert_subtract_fusion), kind=kLoop, calls=%fused_computation.11 | loop fusion | flops 18874368 | bytes 20996096 | tf_op jit(solution)/shard_map/convert_element_type | solution.py:54
  52.9 2.9 collective-permute-start.1
  55.8 91.2 %collective-permute-done.1 = bf16[1024,2048]{1,0:T(8,128)(2,1)} collective-permute-done((bf16[1024,2048]{1,0:T(8,128)(2,1)}, bf16[1024,2048]{1,0:T(8,128)(2,1)}, u32[]{:S(2)}, u32[]{:S(2)}) %collective-permute-start.1) | collective-permute-done | bytes 4194336 | tf_op jit(solution)/shard_map/ppermute | solution.py:10
  147.0 8.5 %maximum_select_fusion = bf16[2,1024,2048]{2,1,0:T(8,128)(2,1)S(1)} fusion(bf16[1,1024,2048]{2,1,0:T(8,128)(2,1)} %bitcast.14, bf16[1,1024,2048]{2,1,0:T(8,128)(2,1)} %bitcast.13, pred[]{:T(512)S(6)} %eq.46), kind=kLoop, calls=%fused_computation.9 | loop fusion | flops 12582912 | bytes 16777216 | tf_op jit(solution)/shard_map/jit(_where)/select_n | solution.py:56
  155.5 0.0 copy-start.2
  155.5 3.2 copy-done.2
  158.7 40.5 %fusion = f32[1024,8192]{1,0:T(8,128)} fusion(bf16[1,2,2048,8192]{3,2,1,0:T(8,128)(2,1)} %param.14, bf16[2,1024,2048]{2,1,0:T(8,128)(2,1)S(1)} %maximum_select_fusion), kind=kOutput, calls=%fused_computation | convolution fusion | flops 34359738368 | bytes 71303168 | tf_op jit(solution)/shard_map/dot_general | solution.py:61
  199.1 47.5 %fusion.6 = f32[1024,8192]{1,0:T(8,128)} fusion(f32[1024,8192]{1,0:T(8,128)} %fusion, bf16[1,2,2048,8192]{3,2,1,0:T(8,128)(2,1)} %param.14, bf16[2,1024,2048]{2,1,0:T(8,128)(2,1)} %copy-done.2), kind=kOutput, calls=%fused_computation.6 | convolution fusion | flops 34368126976 | bytes 104857600 | tf_op jit(solution)/shard_map/dot_general | solution.py:59
  246.6 0.0 copy-start.3
  246.6 0.0 reduce-scatter.2.cloned.1.call-update
  246.6 0.0 copy-start.1
  246.7 544.6 %reduce-scatter.2.cloned.1.call-done = f32[128,8192]{1,0:T(8,128)} async-done(((f32[1024,8192]{1,0:T(8,128)}), f32[128,8192]{1,0:T(8,128)}) %reduce-scatter.2.cloned.1.call-update) | async-done | bytes 4194320 | tf_op jit(solution)/shard_map/reduce_scatter | solution.py:60
  791.3 0.0 copy-done.3
  791.3 3.9 fusion.14
  795.1 0.0 copy-done.1
  (3 shorter events, 0.0 us)
Async XLA Ops:
  6.5 26.1 %copy-start = (f32[16]{0:T(128)S(1)}, f32[16]{0:T(128)}, u32[]{:S(2)}) copy-start(f32[16]{0:T(128)} %param.19) | copy-start | bytes 196
  6.5 24.6 %copy-start.6 = (s32[2,1024]{1,0:T(2,128)S(1)}, s32[2,1024]{1,0:T(2,128)}, u32[]{:S(2)}) copy-start(s32[2,1024]{1,0:T(2,128)} %param.18) | copy-start | bytes 24580
  6.5 24.6 %copy-start.7 = (s32[2,1024]{1,0:T(2,128)S(1)}, s32[2,1024]{1,0:T(2,128)}, u32[]{:S(2)}) copy-start(s32[2,1024]{1,0:T(2,128)} %param.16) | copy-start | bytes 24580
  6.5 24.6 %copy-start.8 = (s32[2,1024]{1,0:T(2,128)S(1)}, s32[2,1024]{1,0:T(2,128)}, u32[]{:S(2)}) copy-start(s32[2,1024]{1,0:T(2,128)} %param.17) | copy-start | bytes 24580
  6.5 28.0 %copy-start.4 = (f32[2,2048]{1,0:T(2,128)S(1)}, f32[2,2048]{1,0:T(2,128)}, u32[]{:S(2)}) copy-start(f32[2,2048]{1,0:T(2,128)} %param.13) | copy-start | bytes 49156
  6.5 28.0 %copy-start.5 = (f32[2,2048]{1,0:T(2,128)S(1)}, f32[2,2048]{1,0:T(2,128)}, u32[]{:S(2)}) copy-start(f32[2,2048]{1,0:T(2,128)} %param.12) | copy-start | bytes 49156
  6.6 784.7 %reduce-scatter.2.cloned.1.call-start = ((), (), s32[]{:S(2)}) async-start(), calls=%async_computation.1 | async-start | bytes 37748736 | tf_op jit(solution)/shard_map/reduce_scatter | solution.py:60
  30.7 13.6 %collective-permute-start = (f32[1024,2048]{1,0:T(8,128)}, f32[1024,2048]{1,0:T(8,128)}, u32[]{:S(2)}, u32[]{:S(2)}) collective-permute-start(f32[1024,2048]{1,0:T(8,128)} %fusion.9), channel_id=1, source_target_pairs={{0,8},{8,0},{16,24},{24,16},{1,9},{9,1},{17,25},{25,17},{2,10},{10... | collective-permute-start | bytes 25165832 | tf_op jit(solution)/shard_map/ppermute | solution.py:10
  52.9 94.1 %collective-permute-start.1 = (bf16[1024,2048]{1,0:T(8,128)(2,1)}, bf16[1024,2048]{1,0:T(8,128)(2,1)}, u32[]{:S(2)}, u32[]{:S(2)}) collective-permute-start(bf16[1024,2048]{1,0:T(8,128)(2,1)} %select_convert_fusion), channel_id=1, source_target_pairs={{0,16},{8,24},{16,0},{24,8},{1,17},{9,25},{17,1},{25,9},{2,18},{10... | collective-permute-start | bytes 12582920 | tf_op jit(solution)/shard_map/ppermute | solution.py:10
  155.5 3.2 copy-start.2
  246.6 544.7 %copy-start.3 = (f32[1,8192]{1,0:T(1,128)S(1)}, f32[1,8192]{1,0:T(1,128)}, u32[]{:S(2)}) copy-start(f32[1,8192]{1,0:T(1,128)} %param.15) | copy-start | bytes 98308
  246.6 548.5 %copy-start.1 = (f32[16]{0:T(128)S(1)}, f32[16]{0:T(128)}, u32[]{:S(2)}) copy-start(f32[16]{0:T(128)} %param.19) | copy-start | bytes 196
Sparse Core Ops, SparseCore 0:
  246.8 544.4 reduce-scatter.1
where the time goes:
time: 802 us
  waiting for transfers between devices  645 us (80%)
  matrix products  115 us (14%)
  other arithmetic  21 us (3%)
  between operations  13.5 us (2%)
    reduce_scatter x1, waiting for transfers between devices, shards(): lax.psum_scatter(total + jnp.dot(both_codes[1], dec_weight[0, 1], preferr...  545 us
    ppermute x2, waiting for transfers between devices, swapped(): return lax.ppermute(value, axis, pairs)  101 us
    dot_general x1, matrix products, shards(): jnp.dot(both_codes[0], dec_weight[0, 0], preferred_element_type=jnp.float32)  47.5 us
    dot_general x1, matrix products, shards(): jnp.dot(both_codes[1], dec_weight[0, 1], preferred_element_type=jnp.float32)  40.5 us
    dot_general x1, matrix products, shards(): jnp.dot(resid_halves[0], enc_weight[0], preferred_element_type=jnp.float32)  24.1 us
  transfers between devices with their start and end apart: 3, of which 3 were waited for; matrix products, arithmetic and copies ran while one was open for 0% of the time, Pallas kernels for 0%

commit v1 on v0

v1 whole, which is shorter than its diff:
```python
import functools

import jax
import jax.numpy as jnp
from jax import lax
from jax.experimental import pallas as pl
from jax.experimental.pallas import tpu as pltpu
from jax.sharding import PartitionSpec as P

MESH = pl.DeviceIdType.MESH
BLOCK = 256
RING = 4
LAG = 3


def swapped(value, axis, distance):
    mask = 2**distance
    pairs = [(source, source ^ mask) for source in range(lax.axis_size(axis))]
    return lax.ppermute(value, axis, pairs)


def decode_kernel(
    n_lat, codes, weight, bias, out,
    wbuf, send1, recv1, kept, send2, recv2, mine,
    w_sem, s1_sem, r1_sem, s2_sem, r2_sem,
):
    outer = n_lat // 2
    rows = out.shape[0]
    steps = out.shape[1] // BLOCK
    me = lax.axis_index("lat")
    side = lax.rem(me, 2)
    place = me // 2
    partner = place * 2 + (1 - side)
    peers = [lax.rem(place + k, outer) * 2 + side for k in range(1, outer)]

    def columns(j):
        return pl.ds(pl.multiple_of(j * BLOCK, BLOCK), BLOCK)

    def load(j):
        return pltpu.make_async_copy(
            weight.at[:, :, columns(j)], wbuf.at[lax.rem(j, 2)], w_sem.at[lax.rem(j, 2)]
        )

    def swap(j):
        slot = lax.rem(j, RING)
        return pltpu.make_async_remote_copy(
            src_ref=send1.at[slot], dst_ref=recv1.at[j],
            send_sem=s1_sem.at[slot], recv_sem=r1_sem.at[j],
            device_id={"lat": partner}, device_id_type=MESH,
        )

    def spread(j, k):
        slot = lax.rem(j, RING)
        return pltpu.make_async_remote_copy(
            src_ref=send2.at[slot, k - 1], dst_ref=recv2.at[j, k - 1],
            send_sem=s2_sem.at[slot, k - 1], recv_sem=r2_sem.at[j, k - 1],
            device_id={"lat": peers[k - 1]}, device_id_type=MESH,
        )

    load(0).start()
    barrier = pltpu.get_barrier_semaphore()
    for device in [partner] + peers:
        pl.semaphore_signal(barrier, inc=1, device_id={"lat": device}, device_id_type=MESH)
    pl.semaphore_wait(barrier, outer)

    def partial(half, slot):
        return jnp.dot(
            codes[0, half], wbuf[slot, 0], preferred_element_type=jnp.float32
        ) + jnp.dot(codes[1, half], wbuf[slot, 1], preferred_element_type=jnp.float32)

    def step(t, carry):
        @pl.when(t < steps)
        def _():
            slot = lax.rem(t, 2)

            @pl.when(t + 1 < steps)
            def _():
                load(t + 1).start()

            load(t).wait()

            @pl.when(t >= RING)
            def _():
                swap(t - RING).wait_send()

            send1[lax.rem(t, RING)] = partial(1 - side, slot).astype(jnp.bfloat16)
            swap(t).start()
            kept[lax.rem(t, RING)] = partial(side, slot)

        u = t - LAG

        @pl.when((u >= 0) & (u < steps))
        def _():
            slot = lax.rem(u, RING)
            swap(u).wait_recv()

            @pl.when(u >= RING)
            def _():
                for k in range(1, outer):
                    spread(u - RING, k).wait_send()

            def total(where):
                span = pl.ds(pl.multiple_of(where * rows, rows), rows)
                return kept[slot, span, :] + recv1[u, span, :].astype(jnp.float32)

            for k in range(1, outer):
                send2[slot, k - 1] = total(lax.rem(place + k, outer)).astype(jnp.bfloat16)
                spread(u, k).start()
            mine[slot] = total(place)

        v = t - 2 * LAG

        @pl.when((v >= 0) & (v < steps))
        def _():
            result = mine[lax.rem(v, RING)] + bias[0, columns(v)][None, :]
            for k in range(1, outer):
                spread(v, k).wait_recv()
                result = result + recv2[v, k - 1].astype(jnp.float32)
            out[:, columns(v)] = result.astype(jnp.bfloat16)

        return carry

    lax.fori_loop(0, steps + 2 * LAG, step, 0)
    for j in range(steps - RING, steps):
        swap(j).wait_send()
        for k in range(1, outer):
            spread(j, k).wait_send()


def decode(codes, weight, bias, n_lat):
    _, _, half_rows, width = codes.shape
    model = weight.shape[2]
    steps = model // BLOCK
    outer = n_lat // 2
    rows = half_rows // outer
    vmem = pl.BlockSpec(memory_space=pltpu.VMEM)
    dma = pltpu.SemaphoreType.DMA
    return pl.pallas_call(
        functools.partial(decode_kernel, n_lat),
        out_shape=jax.ShapeDtypeStruct((rows, model), jnp.bfloat16),
        in_specs=[vmem, pl.BlockSpec(memory_space=pl.ANY), vmem],
        out_specs=vmem,
        scratch_shapes=[
            pltpu.VMEM((2, 2, width, BLOCK), jnp.bfloat16),
            pltpu.VMEM((RING, half_rows, BLOCK), jnp.bfloat16),
            pltpu.VMEM((steps, half_rows, BLOCK), jnp.bfloat16),
            pltpu.VMEM((RING, half_rows, BLOCK), jnp.float32),
            pltpu.VMEM((RING, outer - 1, rows, BLOCK), jnp.bfloat16),
            pltpu.VMEM((steps, outer - 1, rows, BLOCK), jnp.bfloat16),
            pltpu.VMEM((RING, rows, BLOCK), jnp.float32),
            dma((2,)),
            dma((RING,)),
            dma((steps,)),
            dma((RING, outer - 1)),
            dma((steps, outer - 1)),
        ],
        compiler_params=pltpu.CompilerParams(
            collective_id=0, has_side_effects=True, vmem_limit_bytes=54 * 2**20
        ),
        cost_estimate=pl.CostEstimate(
            flops=2 * 2 * half_rows * 2 * width * model,
            bytes_accessed=2 * 2 * width * model,
            transcendentals=0,
        ),
    )(codes, weight, bias)


def by_side(rows, n_lat):
    cut = rows.reshape((n_lat // 2, 2, rows.shape[0] // n_lat) + rows.shape[1:])
    return jnp.swapaxes(cut, 0, 1).reshape((2, rows.shape[0] // 2) + rows.shape[1:])


def shards(
    resid_halves,
    enc_weight,
    enc_bias,
    jump_threshold,
    dec_weight,
    dec_bias,
    clamp_rows,
    clamp_feats,
    clamp_slots,
    clamp_values,
):
    n_lat = lax.axis_size("lat")
    group = lax.axis_index("layer")
    source = group // 2
    core = lax.rem(group, 2)
    tokens = resid_halves.shape[1]
    width = enc_weight.shape[2]
    lat_first = lax.axis_index("lat") * width

    def pick(stacked, at):
        return lax.dynamic_index_in_dim(stacked, at, 0, keepdims=False)

    my_bias = pick(enc_bias, source)
    my_thresh = pick(jump_threshold, source)
    my_slots = pick(clamp_slots, source)
    slot_hot = my_slots[:, None] == jnp.arange(clamp_values.shape[0], dtype=jnp.int32)[None, :]
    chosen = jnp.sum(jnp.where(slot_hot, clamp_values[None, :], 0.0), axis=1)
    row_hot = pick(clamp_rows, source)[:, None] == jnp.arange(tokens, dtype=jnp.int32)[None, :]
    feat_row = jnp.sum(jnp.where(row_hot, pick(clamp_feats, source)[:, None], 0), axis=0)
    value_row = jnp.sum(jnp.where(row_hot, chosen[:, None], 0.0), axis=0)
    feat_row = by_side(feat_row, n_lat)
    value_row = by_side(value_row, n_lat)

    partial_pre = jnp.dot(
        by_side(resid_halves[0], n_lat).reshape(tokens, -1), enc_weight[0],
        preferred_element_type=jnp.float32,
    ).reshape(2, tokens // 2, width)
    partner = swapped(pick(partial_pre, 1 - core), "layer", 0)
    pre_act = pick(partial_pre, core) + partner + my_bias[None, :]
    ramp = jnp.clip((pre_act - my_thresh[None, :]) / 0.25 + 1.0, 0.0, 1.0)
    hit = (pick(feat_row, core) - lat_first)[:, None] == jnp.arange(width, dtype=jnp.int32)[None, :]
    half = jnp.where(hit, pick(value_row, core)[:, None], pre_act * ramp).astype(jnp.bfloat16)
    other = swapped(half, "layer", 1)
    held = jnp.where(source == 0, jnp.stack([half, other]), jnp.stack([other, half]))
    taken = swapped(held, "layer", 0)
    codes = jnp.where(
        core == 0, jnp.stack([held, taken], axis=1), jnp.stack([taken, held], axis=1)
    )
    return decode(codes, dec_weight[0], dec_bias, n_lat)[None]


def solution(mesh):
    return jax.shard_map(
        shards,
        mesh=mesh,
        in_specs=(
            P("layer", None, None),
            P("layer", None, "lat"),
            P(None, "lat"),
            P(None, "lat"),
            P("layer", None, "lat", None),
            P("layer", None),
            P(),
            P(),
            P(),
            P(),
        ),
        out_specs=P("layer", "lat", None),
        check_vma=False,
    )
```

time: 802 us -> 327 us (0.41)
  waiting for transfers between devices: 645 us -> 56.1 us
  Pallas kernels: 0 us -> 209 us
  matrix products: 115 us -> 21 us
  between operations: 13.5 us -> 0.18 us
  local copies, waits for them, and re-layouts: 3.27 us -> 15.3 us
    reduce_scatter x1 -> x0, waiting for transfers between devices: 545 us -> none  [shards(): lax.psum_scatter(total + jnp.dot(both_codes[1], dec_weight[0, 1], preferr...]
    pallas_call x0 -> x1, Pallas kernels: none -> 209 us  [decode(): pl.pallas_call(functools.partial(decode_kernel, n_lat), out_shape=jax.Sha...]
    dot_general x6 -> x1, matrix products: 115 us -> 21 us  [shards(): jnp.dot(by_side(resid_halves[0], n_lat).reshape(tokens, -1), enc_weight[0...]
    ppermute x2 -> x3, waiting for transfers between devices: 101 us -> 56.1 us  [swapped(): return lax.ppermute(value, axis, pairs)]
  transfers between devices with their start and end apart: 3 -> 3, of which waited for: 3 -> 3; matrix products, arithmetic and copies ran while one was open for 0% -> 1% of each run, Pallas kernels for 0% -> 0%
where the time goes in v1:
time: 327 us; the launch traced here: 326 us
  Pallas kernels  209 us (64%)
  waiting for transfers between devices  56.1 us (17%)
  other arithmetic  21.5 us (7%)
  matrix products  21 us (6%)
  local copies, waits for them, and re-layouts  15.3 us (5%)
  starting transfers between devices  3.41 us (1%)
    pallas_call x1, Pallas kernels, decode(): pl.pallas_call(functools.partial(decode_kernel, n_lat), out_shape=jax.Sha...  209 us
    ppermute x3, waiting for transfers between devices, swapped(): return lax.ppermute(value, axis, pairs)  56.1 us
    dot_general x1, matrix products, shards(): jnp.dot(by_side(resid_halves[0], n_lat).reshape(tokens, -1), enc_weight[0...  21 us
    select_n x1, other arithmetic, shards(): jnp.where(core == 0, jnp.stack([held, taken], axis=1), jnp.stack([taken,...  8.24 us
    transpose x1, local copies, waits for them, and re-layouts, by_side(): jnp.swapaxes(cut, 0, 1).reshape((2, rows.shape[0] // 2) + rows.shape[1:])  7.72 us
    select_n x2, other arithmetic, shards(): jnp.where(source == 0, jnp.stack([half, other]), jnp.stack([other, half]))  7.61 us
  transfers between devices with their start and end apart: 3, of which 3 were waited for; matrix products, arithmetic and copies ran while one was open for 1% of the time, Pallas kernels for 0%

profile of v1, /device:TPU:0, one launch (start us, length us, event | category | flops | bytes accessed | tf_op | source)
XLA Modules:
  0.0 326.5 jit_solution(11101521680635879292)
XLA Ops:
  0.0 0.0 copy-start
  0.0 7.7 %copy.12 = bf16[2,4,128,4096]{3,2,1,0:T(8,128)(2,1)} copy(bf16[2,4,128,4096]{3,2,0,1:T(8,128)(2,1)} %bitcast.43) | data formatting | bytes 16777216 | tf_op jit(solution)/shard_map/transpose | solution.py:170
  7.7 21.0 %fusion = f32[2,512,2048]{2,1,0:T(8,128)S(1)} fusion(bf16[2,512,4096]{2,1,0:T(8,128)(2,1)} %bitcast.44, bf16[1,4096,2048]{2,1,0:T(8,128)(2,1)} %param.11), kind=kOutput, calls=%fused_computation | convolution fusion | flops 17179869184 | bytes 33554432 | tf_op jit(solution)/shard_map/dot_general | solution.py:207
  28.8 0.0 copy-start.2
  28.8 0.0 copy-start.5
  28.8 0.0 copy-start.6
  28.8 0.0 copy-start.7
  28.8 0.0 copy-start.3
  28.8 0.0 copy-start.4
  28.8 2.5 dynamic-slice_bitcast_fusion
  31.3 2.0 copy-done.2
  33.3 0.5 collective-permute-start
  33.7 0.0 copy-done
  33.7 0.0 copy-done.5
  33.7 0.0 copy-done.6
  33.8 0.0 copy-done.7
  33.8 0.1 select_reduce_fusion.2
  33.9 0.5 select_reduce_fusion
  34.5 0.7 select_reduce_fusion.1
  35.1 0.0 copy-done.3
  35.2 0.0 copy-done.4
  35.2 5.7 %collective-permute-done = f32[512,2048]{1,0:T(8,128)} collective-permute-done((f32[512,2048]{1,0:T(8,128)}, f32[512,2048]{1,0:T(8,128)}, u32[]{:S(2)}, u32[]{:S(2)}) %collective-permute-start) | collective-permute-done | bytes 4194336 | tf_op jit(solution)/shard_map/ppermute | solution.py:19
  40.9 4.3 %select_convert_fusion = bf16[512,2048]{1,0:T(8,128)(2,1)S(1)} fusion(f32[512,2048]{1,0:T(8,128)} %collective-permute-done, f32[2,512,2048]{2,1,0:T(8,128)} %copy-done.2, s32[]{:T(128)S(6)} %select_n.73, f32[2048]{0:T(1024)S(1)} %bitcast.49, f32[2048]{0:T(1024)S(1)} %bitcast.48, f32[512]{0:T(512)S(1)} %bitcast.54, s32[512]{0:T(512)S(1)} %bitcast.55), kind=kLoop, calls=%fused_computation.7 | loop fusion | flops 9437184 | bytes 10506244 | tf_op jit(solution)/shard_map/convert_element_type | solution.py:215
  45.2 3.0 collective-permute-start.1
  48.1 46.0 %collective-permute-done.1 = bf16[512,2048]{1,0:T(8,128)(2,1)} collective-permute-done((bf16[512,2048]{1,0:T(8,128)(2,1)S(1)}, bf16[512,2048]{1,0:T(8,128)(2,1)}, u32[]{:S(2)}, u32[]{:S(2)}) %collective-permute-start.1) | collective-permute-done | bytes 2097184 | tf_op jit(solution)/shard_map/ppermute | solution.py:19
  94.2 4.5 %maximum_select_fusion.2 = bf16[2,512,2048]{2,1,0:T(8,128)(2,1)} fusion(bf16[1,512,2048]{2,1,0:T(8,128)(2,1)} %bitcast.23, bf16[1,512,2048]{2,1,0:T(8,128)(2,1)S(1)} %bitcast.41, pred[]{:T(512)S(6)} %eq.50), kind=kLoop, calls=%fused_computation.4 | loop fusion | flops 6291456 | bytes 8388609 | tf_op jit(solution)/shard_map/jit(_where)/select_n | solution.py:217
  98.7 0.0 collective-permute-start.2
  98.7 3.1 maximum_select_fusion.1
  101.8 4.4 %collective-permute-done.2 = bf16[2,512,2048]{2,1,0:T(8,128)(2,1)} collective-permute-done((bf16[2,512,2048]{2,1,0:T(8,128)(2,1)}, bf16[2,512,2048]{2,1,0:T(8,128)(2,1)}, u32[]{:S(2)}, u32[]{:S(2)}) %collective-permute-start.2) | collective-permute-done | bytes 4194336 | tf_op jit(solution)/shard_map/ppermute | solution.py:19
  106.2 8.2 %maximum_select_fusion.codes = bf16[2,2,512,2048]{3,2,1,0:T(8,128)(2,1)} fusion(bf16[2,1,512,2048]{3,2,1,0:T(8,128)(2,1)} %bitcast.24, bf16[2,1,512,2048]{3,2,1,0:T(8,128)(2,1)S(1)} %maximum_select_fusion.1, pred[]{:T(512)S(6)} %eq.49), kind=kLoop, calls=%fused_computation.2 | loop fusion | flops 12582912 | bytes 16777216 | tf_op jit(solution)/shard_map/jit(_where)/select_n | solution.py:219
  114.4 0.0 copy-start.1
  114.4 208.9 %shard_map.100 = bf16[128,8192]{1,0:T(8,128)(2,1)} custom-call(bf16[2,2,512,2048]{3,2,1,0:T(8,128)(2,1)} %maximum_select_fusion.codes, bf16[2,2048,8192]{2,1,0:T(8,128)(2,1)} %bitcast.25.weight, f32[1,8192]{1,0:T(1,128)} %bias.1), custom_call_target="tpu_custom_call" | custom-call | flops 68719476736 | bytes 67108864 | tf_op jit(solution)/shard_map/pallas_call | solution.py:138
  323.4 3.1 copy.14
  326.5 0.0 copy-done.1
  (5 shorter events, 0.1 us)
Async XLA Ops:
  0.0 33.7 %copy-start = (s32[2,1024]{1,0:T(2,128)S(1)}, s32[2,1024]{1,0:T(2,128)}, u32[]{:S(2)}) copy-start(s32[2,1024]{1,0:T(2,128)} %param.16) | copy-start | bytes 24580
  28.8 4.5 %copy-start.2 = (f32[2,512,2048]{2,1,0:T(8,128)}, f32[2,512,2048]{2,1,0:T(8,128)S(1)}, u32[]{:S(2)}) copy-start(f32[2,512,2048]{2,1,0:T(8,128)S(1)} %fusion) | copy-start | bytes 25165828
  28.8 5.0 %copy-start.5 = (s32[2,1024]{1,0:T(2,128)S(1)}, s32[2,1024]{1,0:T(2,128)}, u32[]{:S(2)}) copy-start(s32[2,1024]{1,0:T(2,128)} %param.18) | copy-start | bytes 24580
  28.8 5.0 %copy-start.6 = (s32[2,1024]{1,0:T(2,128)S(1)}, s32[2,1024]{1,0:T(2,128)}, u32[]{:S(2)}) copy-start(s32[2,1024]{1,0:T(2,128)} %param.17) | copy-start | bytes 24580
  28.8 5.0 %copy-start.7 = (f32[16]{0:T(128)S(1)}, f32[16]{0:T(128)}, u32[]{:S(2)}) copy-start(f32[16]{0:T(128)} %param.19) | copy-start | bytes 196
  28.8 6.3 %copy-start.3 = (f32[2,2048]{1,0:T(2,128)S(1)}, f32[2,2048]{1,0:T(2,128)}, u32[]{:S(2)}) copy-start(f32[2,2048]{1,0:T(2,128)} %param.12) | copy-start | bytes 49156
  28.8 6.3 %copy-start.4 = (f32[2,2048]{1,0:T(2,128)S(1)}, f32[2,2048]{1,0:T(2,128)}, u32[]{:S(2)}) copy-start(f32[2,2048]{1,0:T(2,128)} %param.13) | copy-start | bytes 49156
  33.3 7.6 %collective-permute-start = (f32[512,2048]{1,0:T(8,128)}, f32[512,2048]{1,0:T(8,128)}, u32[]{:S(2)}, u32[]{:S(2)}) collective-permute-start(f32[512,2048]{1,0:T(8,128)} %dynamic-slice_bitcast_fusion), channel_id=1, source_target_pairs={{0,8},{8,0},{16,24},{24,16},{1,9},{9,1},{17,25},{25,17},{2,10},{10... | collective-permute-start | bytes 12582920 | tf_op jit(solution)/shard_map/ppermute | solution.py:19
  45.2 49.0 %collective-permute-start.1 = (bf16[512,2048]{1,0:T(8,128)(2,1)S(1)}, bf16[512,2048]{1,0:T(8,128)(2,1)}, u32[]{:S(2)}, u32[]{:S(2)}) collective-permute-start(bf16[512,2048]{1,0:T(8,128)(2,1)S(1)} %select_convert_fusion), channel_id=1, source_target_pairs={{0,16},{8,24},{16,0},{24,8},{1,17},{9,25},{17,1},{25,9},{2,18},{10... | collective-permute-start | bytes 6291464 | tf_op jit(solution)/shard_map/ppermute | solution.py:19
  98.7 7.5 %collective-permute-start.2 = (bf16[2,512,2048]{2,1,0:T(8,128)(2,1)}, bf16[2,512,2048]{2,1,0:T(8,128)(2,1)}, u32[]{:S(2)}, u32[]{:S(2)}) collective-permute-start(bf16[2,512,2048]{2,1,0:T(8,128)(2,1)} %maximum_select_fusion.2), channel_id=1, source_target_pairs={{0,8},{8,0},{16,24},{24,16},{1,9},{9,1},{17,25},{25,17},{2,10},{10... | collective-permute-start | bytes 12582920 | tf_op jit(solution)/shard_map/ppermute | solution.py:19
  114.4 212.0 %copy-start.1 = (s32[2,1024]{1,0:T(2,128)S(1)}, s32[2,1024]{1,0:T(2,128)}, u32[]{:S(2)}) copy-start(s32[2,1024]{1,0:T(2,128)} %param.16) | copy-start | bytes 24580

commit v2 on v0

v2 whole, which is shorter than its diff:
```python
import functools

import jax
import jax.numpy as jnp
from jax import lax
from jax.experimental import pallas as pl
from jax.experimental.pallas import tpu as pltpu
from jax.sharding import PartitionSpec as P

MESH = pl.DeviceIdType.MESH
PASSES = 2
BLOCK = 512
RING = 4
LAG = 3


def swapped(value, axis, distance):
    mask = 2**distance
    pairs = [(source, source ^ mask) for source in range(lax.axis_size(axis))]
    return lax.ppermute(value, axis, pairs)


def decode_kernel(stages, half, weight, bias, out, *scratch):
    codes, wbuf, own_sem, w_sem, give_sem, take_sem = scratch[:6]
    kept, sent, got, s_sem, r_sem = (scratch[6 + i * stages : 6 + (i + 1) * stages] for i in range(5))
    rows = out.shape[0] // PASSES
    blocks = out.shape[1] // BLOCK
    steps = PASSES * blocks
    me = lax.axis_index("lat")
    group = lax.axis_index("layer")
    source, core = group // 2, lax.rem(group, 2)
    sibling = source * 2 + (1 - core)
    across = (1 - source) * 2 + core
    bits = [lax.rem(me // 2**i, 2) for i in range(stages)]
    mates = [me + (1 - 2 * bits[i]) * 2**i for i in range(stages)]

    def columns(t):
        return pl.ds(pl.multiple_of(lax.rem(t, blocks) * BLOCK, BLOCK), BLOCK)

    def load(t):
        return pltpu.make_async_copy(
            weight.at[:, :, columns(t)], wbuf.at[lax.rem(t, 2)], w_sem.at[lax.rem(t, 2)]
        )

    def settle(p):
        return pltpu.make_async_copy(half.at[p], codes.at[p, source, core], own_sem.at[p])

    def give(p, kind):
        of, to = ((source, sibling), (source, across), (1 - source, sibling))[kind]
        piece = codes.at[p, of, core]
        return pltpu.make_async_remote_copy(
            src_ref=piece, dst_ref=piece,
            send_sem=give_sem.at[p, kind], recv_sem=take_sem.at[p, kind],
            device_id={"layer": to}, device_id_type=MESH,
        )

    def take(p, kind):
        of, side = ((source, 1 - core), (1 - source, core), (1 - source, 1 - core))[kind]
        piece = codes.at[p, of, side]
        return pltpu.make_async_remote_copy(
            src_ref=piece, dst_ref=piece,
            send_sem=give_sem.at[p, kind], recv_sem=take_sem.at[p, kind],
            device_id={"layer": sibling}, device_id_type=MESH,
        )

    def pass_on(t, i):
        slot = lax.rem(t, RING)
        return pltpu.make_async_remote_copy(
            src_ref=sent[i].at[slot], dst_ref=got[i].at[t],
            send_sem=s_sem[i].at[slot], recv_sem=r_sem[i].at[t],
            device_id={"lat": mates[i]}, device_id_type=MESH,
        )

    for p in range(PASSES):
        settle(p).start()
    load(0).start()
    barrier = pltpu.get_barrier_semaphore()
    for device in [{"lat": mate} for mate in mates] + [{"layer": sibling}, {"layer": across}]:
        pl.semaphore_signal(barrier, inc=1, device_id=device, device_id_type=MESH)
    pl.semaphore_wait(barrier, stages + 2)

    settle(0).wait()
    give(0, 1).start()
    give(0, 0).start()
    settle(1).wait()
    take(0, 1).wait_recv()
    give(0, 2).start()
    give(1, 1).start()
    give(1, 0).start()
    take(0, 0).wait_recv()
    take(0, 2).wait_recv()

    def step(t, carry):
        @pl.when(t == blocks // 2)
        def _():
            take(1, 1).wait_recv()
            give(1, 2).start()

        @pl.when(t == blocks)
        def _():
            take(1, 0).wait_recv()
            take(1, 2).wait_recv()

        @pl.when(t < steps)
        def _():
            slot, p = lax.rem(t, 2), t // blocks

            def partial(side):
                return jnp.dot(
                    codes[p, 0, side], wbuf[slot, 0], preferred_element_type=jnp.float32
                ) + jnp.dot(codes[p, 1, side], wbuf[slot, 1], preferred_element_type=jnp.float32)

            @pl.when(t + 1 < steps)
            def _():
                load(t + 1).start()

            load(t).wait()

            @pl.when(t >= RING)
            def _():
                pass_on(t - RING, 0).wait_send()

            sent[0][lax.rem(t, RING)] = partial(1 - bits[0]).astype(jnp.bfloat16)
            pass_on(t, 0).start()
            kept[0][lax.rem(t, RING)] = partial(bits[0])

        for i in range(1, stages + 1):
            u = t - i * LAG

            @pl.when((u >= 0) & (u < steps))
            def _(i=i, u=u):
                slot = lax.rem(u, RING)
                pass_on(u, i - 1).wait_recv()

                def total(bit, size):
                    span = pl.ds(pl.multiple_of(bit * size, size), size)
                    return kept[i - 1][slot, span, :] + got[i - 1][u, span, :].astype(jnp.float32)

                if i < stages:
                    size = kept[i].shape[1]

                    @pl.when(u >= RING)
                    def _():
                        pass_on(u - RING, i).wait_send()

                    sent[i][slot] = total(1 - bits[i], size).astype(jnp.bfloat16)
                    pass_on(u, i).start()
                    kept[i][slot] = total(bits[i], size)
                else:
                    span = pl.ds(pl.multiple_of((u // blocks) * rows, rows), rows)
                    result = total(0, rows) + bias[0, columns(u)][None, :]
                    out[span, columns(u)] = result.astype(jnp.bfloat16)

        return carry

    lax.fori_loop(0, steps + stages * LAG, step, 0)
    for i in range(stages):
        for t in range(steps - RING, steps):
            pass_on(t, i).wait_send()
    for p in range(PASSES):
        for kind in range(3):
            give(p, kind).wait_send()


def decode(half, weight, bias, n_lat):
    _, part, width = half.shape
    model = weight.shape[2]
    steps = PASSES * (model // BLOCK)
    stages = n_lat.bit_length() - 1
    rows = PASSES * 2 * part // n_lat
    sizes = [part // 2**i for i in range(stages)]
    dma = pltpu.SemaphoreType.DMA
    vmem = pl.BlockSpec(memory_space=pltpu.VMEM)
    hbm = pl.BlockSpec(memory_space=pl.ANY)
    return pl.pallas_call(
        functools.partial(decode_kernel, stages),
        out_shape=jax.ShapeDtypeStruct((rows, model), jnp.bfloat16),
        in_specs=[hbm, hbm, vmem],
        out_specs=vmem,
        scratch_shapes=[
            pltpu.VMEM((PASSES, 2, 2, part, width), jnp.bfloat16),
            pltpu.VMEM((2, 2, width, BLOCK), jnp.bfloat16),
            dma((PASSES,)),
            dma((2,)),
            dma((PASSES, 3)),
            dma((PASSES, 3)),
            *(pltpu.VMEM((RING, size, BLOCK), jnp.float32) for size in sizes),
            *(pltpu.VMEM((RING, size, BLOCK), jnp.bfloat16) for size in sizes),
            *(pltpu.VMEM((steps, size, BLOCK), jnp.bfloat16) for size in sizes),
            *(dma((RING,)) for _ in sizes),
            *(dma((steps,)) for _ in sizes),
        ],
        compiler_params=pltpu.CompilerParams(
            collective_id=0, has_side_effects=True, vmem_limit_bytes=54 * 2**20
        ),
        cost_estimate=pl.CostEstimate(
            flops=2 * 2 * PASSES * part * 2 * width * model,
            bytes_accessed=PASSES * 2 * 2 * width * model,
            transcendentals=0,
        ),
    )(half, weight, bias)


def of_side(values, n_lat, side):
    stages = n_lat.bit_length() - 1
    tail = values.shape[1:]
    rows = values.shape[0] // n_lat // PASSES
    cut = values.reshape((n_lat // 2, 2, PASSES * rows) + tail)
    cut = lax.dynamic_index_in_dim(cut, side, 1, keepdims=False)
    cut = cut.reshape((2,) * (stages - 1) + (PASSES, rows) + tail)
    order = (stages - 1,) + tuple(range(stages - 2, -1, -1)) + tuple(range(stages, cut.ndim))
    return cut.transpose(order).reshape((PASSES * rows * n_lat // 2,) + tail)


def shards(
    resid_halves,
    enc_weight,
    enc_bias,
    jump_threshold,
    dec_weight,
    dec_bias,
    clamp_rows,
    clamp_feats,
    clamp_slots,
    clamp_values,
):
    n_lat = lax.axis_size("lat")
    group = lax.axis_index("layer")
    source = group // 2
    core = lax.rem(group, 2)
    tokens = resid_halves.shape[1]
    width = enc_weight.shape[2]
    lat_first = lax.axis_index("lat") * width

    def pick(stacked, at):
        return lax.dynamic_index_in_dim(stacked, at, 0, keepdims=False)

    my_bias = pick(enc_bias, source)
    my_thresh = pick(jump_threshold, source)
    my_slots = pick(clamp_slots, source)
    slot_hot = my_slots[:, None] == jnp.arange(clamp_values.shape[0], dtype=jnp.int32)[None, :]
    chosen = jnp.sum(jnp.where(slot_hot, clamp_values[None, :], 0.0), axis=1)
    row_hot = pick(clamp_rows, source)[:, None] == jnp.arange(tokens, dtype=jnp.int32)[None, :]
    feat_row = jnp.sum(jnp.where(row_hot, pick(clamp_feats, source)[:, None], 0), axis=0)
    value_row = jnp.sum(jnp.where(row_hot, chosen[:, None], 0.0), axis=0)
    feat_row = of_side(feat_row, n_lat, core)
    value_row = of_side(value_row, n_lat, core)

    partial_pre = jnp.dot(resid_halves[0], enc_weight[0], preferred_element_type=jnp.float32)
    partner = swapped(of_side(partial_pre, n_lat, 1 - core), "layer", 0)
    pre_act = of_side(partial_pre, n_lat, core) + partner + my_bias[None, :]
    ramp = jnp.clip((pre_act - my_thresh[None, :]) / 0.25 + 1.0, 0.0, 1.0)
    hit = (feat_row - lat_first)[:, None] == jnp.arange(width, dtype=jnp.int32)[None, :]
    half = jnp.where(hit, value_row[:, None], pre_act * ramp).astype(jnp.bfloat16)
    half = half.reshape(PASSES, tokens // 2 // PASSES, width)
    return decode(half, dec_weight[0], dec_bias, n_lat)[None]


def solution(mesh):
    return jax.shard_map(
        shards,
        mesh=mesh,
        in_specs=(
            P("layer", None, None),
            P("layer", None, "lat"),
            P(None, "lat"),
            P(None, "lat"),
            P("layer", None, "lat", None),
            P("layer", None),
            P(),
            P(),
            P(),
            P(),
        ),
        out_specs=P("layer", "lat", None),
        check_vma=False,
    )
```

time: 802 us -> 275 us (0.34)
  waiting for transfers between devices: 645 us -> 0.59 us
  Pallas kernels: 0 us -> 233 us
  matrix products: 115 us -> 21.4 us
  other arithmetic: 21 us -> 6.59 us
  between operations: 13.5 us -> 0.09 us
  local copies, waits for them, and re-layouts: 3.27 us -> 13.3 us
    reduce_scatter x1 -> x0, waiting for transfers between devices: 545 us -> none  [shards(): lax.psum_scatter(total + jnp.dot(both_codes[1], dec_weight[0, 1], preferr...]
    pallas_call x0 -> x1, Pallas kernels: none -> 233 us  [decode(): pl.pallas_call(functools.partial(decode_kernel, stages), out_shape=jax.Sh...]
    ppermute x2 -> x1, waiting for transfers between devices: 101 us -> 0.59 us  [swapped(): return lax.ppermute(value, axis, pairs)]
    dot_general x5 -> x0, matrix products: 91.3 us -> none  [the longest x1 47.5 us: shards(): jnp.dot(both_codes[0], dec_weight[0, 0], preferred_element_type=jnp.float32)]
    select_n x1 -> x0, other arithmetic: 8.45 us -> none  [shards(): jnp.where(source == 0, jnp.stack([own_codes, other_codes]), jnp.stack([ot...]
  transfers between devices with their start and end apart: 3 -> 1, of which waited for: 3 -> 1; matrix products, arithmetic and copies ran while one was open for 0% -> 2% of each run, Pallas kernels for 0% -> 0%
where the time goes in v2:
time: 275 us
  Pallas kernels  233 us (85%)
  matrix products  21.4 us (8%)
  local copies, waits for them, and re-layouts  13.3 us (5%)
  other arithmetic  6.59 us (2%)
    pallas_call x1, Pallas kernels, decode(): pl.pallas_call(functools.partial(decode_kernel, stages), out_shape=jax.Sh...  233 us
    dot_general x1, matrix products, shards(): jnp.dot(resid_halves[0], enc_weight[0], preferred_element_type=jnp.float32)  21.4 us
    transpose x3, local copies, waits for them, and re-layouts, of_side(): return cut.transpose(order).reshape((PASSES * rows * n_lat // 2,) + tail)  6.95 us
  transfers between devices with their start and end apart: 1, of which 1 were waited for; matrix products, arithmetic and copies ran while one was open for 2% of the time, Pallas kernels for 0%

profile of v2, /device:TPU:0, one launch (start us, length us, event | category | flops | bytes accessed | tf_op | source)
XLA Modules:
  0.0 275.3 jit_solution(3688190630569909040)
XLA Ops:
  0.0 0.0 copy-start
  0.0 21.4 %fusion = f32[4,2,128,2048]{3,2,1,0:T(8,128)S(1)} fusion(bf16[4,2,128,4096]{3,2,1,0:T(8,128)(2,1)} %bitcast.48, bf16[1,4096,2048]{2,1,0:T(8,128)(2,1)} %param.11), kind=kOutput, calls=%fused_computation | convolution fusion | flops 17179869184 | bytes 33554432 | tf_op jit(solution)/shard_map/dot_general | solution.py:249
  21.5 2.8 %constant_dynamic-slice_fusion.3 = (f32[4,1,128,2048]{3,2,1,0:T(8,128)}, f32[4,1,128,2048]{3,2,1,0:T(8,128)S(1)}) fusion(f32[4,2,128,2048]{3,2,1,0:T(8,128)S(1)} %fusion, s32[]{:T(128)S(6)} %select_n.44, s32[]{:T(128)S(6)} %select_n.47), kind=kLoop, calls=%fused_computation.14 | loop fusion | bytes 16777224 | tf_op jit(solution)/shard_map/jit(dynamic_index_in_dim)/dynamic_slice | solution.py:209
  24.2 2.2 copy.22
  26.5 0.5 collective-permute-start
  26.9 0.0 copy-start.3
  26.9 0.0 copy-start.4
  26.9 0.0 copy-start.5
  26.9 0.0 copy-start.1
  26.9 0.0 copy-start.2
  26.9 4.7 %copy.21 = f32[2,2,2,64,2048]{4,3,2,1,0:T(8,128)} copy(f32[2,2,2,64,2048]{4,3,0,1,2:T(8,128)} %bitcast.34) | data formatting | bytes 8388608 | tf_op jit(solution)/shard_map/transpose | solution.py:212
  31.6 0.0 copy-done
  31.7 0.0 copy-done.3
  31.7 0.0 copy-done.4
  31.7 0.7 select_reduce_fusion.1
  32.4 0.1 sub.39
  32.5 0.1 sub.41
  32.6 0.0 copy-done.5
  32.6 0.1 select_reduce_fusion.2
  32.7 0.5 select_reduce_fusion
  33.3 0.1 reshape.54
  33.3 0.1 broadcast_in_dim.69
  33.4 0.0 copy-done.1
  33.4 0.0 copy-done.2
  33.5 0.6 collective-permute-done
  34.1 5.3 %select_convert_fusion = bf16[512,2048]{1,0:T(8,128)(2,1)} fusion(f32[512,2048]{1,0:T(8,128)} %collective-permute-done, f32[2,2,2,64,2048]{4,3,2,1,0:T(8,128)} %copy.21, f32[2048]{0:T(1024)S(1)} %bitcast.40, f32[2048]{0:T(1024)S(1)} %bitcast.41, bf16[512]{0:T(512)(128)(2,1)S(1)} %broadcast_in_dim.69, s32[512]{0:T(512)S(1)} %sub.41), kind=kLoop, calls=%fused_computation.4 | loop fusion | flops 9437184 | bytes 10505216 | tf_op jit(solution)/shard_map/convert_element_type | solution.py:254
  39.3 232.8 %shard_map.100 = bf16[128,8192]{1,0:T(8,128)(2,1)} custom-call(bf16[2,256,2048]{2,1,0:T(8,128)(2,1)} %bitcast.37, bf16[2,2048,8192]{2,1,0:T(8,128)(2,1)} %bitcast.20.weight, f32[1,8192]{1,0:T(1,128)} %bias.1), custom_call_target="tpu_custom_call" | custom-call | flops 68719476736 | bytes 134217728 | tf_op jit(solution)/shard_map/pallas_call | solution.py:175
  272.2 3.1 %copy.25 = bf16[1,128,8192]{2,1,0:T(8,128)(2,1)} copy(bf16[1,128,8192]{2,1,0:T(8,128)(2,1)} %bitcast.36) | data formatting | bytes 4194304
  (7 shorter events, 0.1 us)
Async XLA Ops:
  0.0 31.6 %copy-start = (s32[2,1024]{1,0:T(2,128)S(1)}, s32[2,1024]{1,0:T(2,128)}, u32[]{:S(2)}) copy-start(s32[2,1024]{1,0:T(2,128)} %param.16) | copy-start | bytes 24580
  26.5 7.6 %collective-permute-start = (f32[512,2048]{1,0:T(8,128)}, f32[512,2048]{1,0:T(8,128)}, u32[]{:S(2)}, u32[]{:S(2)}) collective-permute-start(f32[512,2048]{1,0:T(8,128)} %bitcast.16), channel_id=1, source_target_pairs={{0,8},{8,0},{16,24},{24,16},{1,9},{9,1},{17,25},{25,17},{2,10},{10... | collective-permute-start | bytes 12582920 | tf_op jit(solution)/shard_map/ppermute | solution.py:20
  26.9 4.7 %copy-start.3 = (s32[2,1024]{1,0:T(2,128)S(1)}, s32[2,1024]{1,0:T(2,128)}, u32[]{:S(2)}) copy-start(s32[2,1024]{1,0:T(2,128)} %param.18) | copy-start | bytes 24580
  26.9 4.7 %copy-start.4 = (s32[2,1024]{1,0:T(2,128)S(1)}, s32[2,1024]{1,0:T(2,128)}, u32[]{:S(2)}) copy-start(s32[2,1024]{1,0:T(2,128)} %param.17) | copy-start | bytes 24580
  26.9 5.7 %copy-start.5 = (f32[16]{0:T(128)S(1)}, f32[16]{0:T(128)}, u32[]{:S(2)}) copy-start(f32[16]{0:T(128)} %param.19) | copy-start | bytes 196
  26.9 6.5 %copy-start.1 = (f32[2,2048]{1,0:T(2,128)S(1)}, f32[2,2048]{1,0:T(2,128)}, u32[]{:S(2)}) copy-start(f32[2,2048]{1,0:T(2,128)} %param.13) | copy-start | bytes 49156
  26.9 6.5 %copy-start.2 = (f32[2,2048]{1,0:T(2,128)S(1)}, f32[2,2048]{1,0:T(2,128)}, u32[]{:S(2)}) copy-start(f32[2,2048]{1,0:T(2,128)} %param.12) | copy-start | bytes 49156
